TPU v7x, 32 devices: a whole 2x2x4 slice. The times are simulated.
32 devices in a mesh: bead: 4 (over y, x), slab: 8 (over z, core).
Axes of the slice: x: 2, y: 2, z: 4, core: 2. Of those that a mesh axis runs over, the one named last changes fastest.
Arguments:
- section_modes: float32 [3, 8, 4096], P(None, 'bead', 'slab'), may hold values from -3 to 3
- velocity: float32 [3, 8, 4096], P(None, 'bead', 'slab'), may hold values from -6 to 6
- acceleration: float32 [3, 8, 4096], P(None, 'bead', 'slab'), may hold values from -6 to 6
- species: int32 [4096], P('slab'), may hold values from 0 to 1
- neighbours: int32 [32, 4096], P(None, 'slab'), may hold values from 0 to 896, as said below
- ghost_send: int32 [8, 384], P('slab'), may hold values from 0 to 511
Outputs:
- next_modes: float32 [3, 8, 4096], P(None, 'bead', 'slab')
- next_velocity: float32 [3, 8, 4096], P(None, 'bead', 'slab')
- next_acceleration: float32 [3, 8, 4096], P(None, 'bead', 'slab')
Inputs may be any that keep to these rules, and one draw needn't show every extreme that they name: `neighbours`: A slot names the left neighbour slab's ghost block (192 entries), then the slab's own 512 atoms, then the right neighbour's ghost block; the value 512 + 2 * 192 marks an empty slot. `ghost_send`: row s lists first the 192 atoms of slab s that slab s - 1 holds as ghosts, then the 192 atoms that slab s + 1 holds.
All inputs are finite; a program needn't handle non-finite values.
Results may differ from a plain program's by a relative error of at most 0.000092.
Values sent between devices are 32-bit elements; how exact they have to be, the bound alone decides.
A program may use at most 64 MiB of HBM per device.

v0:
```python
import math

import jax
import jax.numpy as jnp
import numpy as np
from jax import lax
from jax.sharding import PartitionSpec as P

step_dt = 0.1
spring = 6.0
alpha_shape = 0.3
beta_shape = 0.5


def with_halo(value, sides, width):
    for axis, dim in sides:
        size, length = (lax.axis_size(axis), value.shape[dim])
        up = [(i, (i + 1) % size) for i in range(size)]
        down = [(j, i) for i, j in up]
        last = lax.slice_in_dim(value, length - width, length, axis=dim)
        leading = lax.slice_in_dim(value, 0, width, axis=dim)
        before = lax.ppermute(last, axis, up)
        after = lax.ppermute(leading, axis, down)
        value = jnp.concatenate([before, value, after], axis=dim)
    return value


def sectioning_inverse(number):
    row_table = np.zeros((number, number))
    row_table[0, 0] = 1.0
    for mode_level in range(number - 1, 0, -1):
        upper_row = row_table[0] if mode_level + 1 == number else row_table[mode_level + 1]
        row_table[mode_level] = (
            mode_level / (mode_level + 1.0) * upper_row + 1.0 / (mode_level + 1.0) * row_table[0]
        )
        row_table[mode_level, mode_level] += 1.0
    return row_table


def force_matrix(number):
    inverse = sectioning_inverse(number)
    weights = np.array([1.0] + [mode_level / (mode_level + 1.0) for mode_level in range(1, number)])
    return weights[:, None] * inverse.T / number


def species_values(species, light_value, heavy_value):
    return jnp.where(species == 1, heavy_value, light_value).astype(jnp.float32)


def propagate(mode_rows, velocity, acceleration, first_mode):
    half_kick = velocity + 0.5 * step_dt * acceleration
    turn_angle = spring * step_dt
    cosine = math.cos(turn_angle)
    sine_turn = math.sin(turn_angle)
    new_modes = jnp.where(
        first_mode,
        mode_rows + step_dt * half_kick,
        cosine * mode_rows + sine_turn / spring * half_kick,
    )
    turned = jnp.where(first_mode, half_kick, cosine * half_kick - spring * sine_turn * mode_rows)
    return (new_modes, turned)


def across_beads(values, matrix):
    mixed_rows = jnp.einsum(
        "kj,cjn->ckn",
        matrix,
        lax.all_to_all(values, "bead", split_axis=2, concat_axis=1, tiled=True),
        precision=lax.Precision.HIGHEST,
    )
    return lax.all_to_all(mixed_rows, "bead", split_axis=1, concat_axis=2, tiled=True)


def ghost_block(block_rows, local_beads, ghost_count):
    place_rows = block_rows[:-1].reshape(3, local_beads, ghost_count)
    amp_row = block_rows[-1]
    rep_row = jnp.where(amp_row > 1.0, 1.5, 0.8).astype(jnp.float32)
    shape_one = (1, local_beads, ghost_count)
    return jnp.concatenate(
        [
            place_rows,
            jnp.broadcast_to(amp_row[None, None, :], shape_one),
            jnp.broadcast_to(rep_row[None, None, :], shape_one),
        ],
        axis=0,
    )


def shards(section_modes, velocity, acceleration, species, neighbours, ghost_send):
    local_beads = section_modes.shape[1]
    atom_count = section_modes.shape[2]
    ghost_count = ghost_send.shape[1] // 2
    slot_span = atom_count + 2 * ghost_count
    number = local_beads * lax.axis_size("bead")
    bead_ids = lax.axis_index("bead") * local_beads + jnp.arange(local_beads, dtype=jnp.int32)
    first_mode = (bead_ids == 0)[None, :, None]
    new_modes, turned = propagate(section_modes, velocity, acceleration, first_mode)
    inverse = jnp.asarray(sectioning_inverse(number), jnp.float32)
    positions = across_beads(new_modes, inverse)
    amplitude = species_values(species, 0.6, 1.4)
    repulsion = species_values(species, 0.8, 1.5)
    embedding = species_values(species, 1.0, 2.5)
    inverse_mass = species_values(species, 1.0, 1.0 / 106.0)
    outgoing = ghost_send[0]
    row_shape = (1, local_beads, atom_count)
    local_rows = jnp.concatenate(
        [
            positions,
            jnp.broadcast_to(amplitude[None, None, :], row_shape),
            jnp.broadcast_to(repulsion[None, None, :], row_shape),
        ],
        axis=0,
    )
    sent_rows = jnp.concatenate(
        [
            jnp.take(positions, outgoing, axis=2).reshape(3 * local_beads, 2 * ghost_count),
            jnp.take(amplitude, outgoing)[None, :],
        ],
        axis=0,
    )
    beside_all = with_halo(sent_rows, (("slab", 1),), ghost_count)
    left_rows = ghost_block(beside_all[:, :ghost_count], local_beads, ghost_count)
    right_rows = ghost_block(beside_all[:, 3 * ghost_count :], local_beads, ghost_count)
    spare_col = jnp.zeros((5, local_beads, 1), jnp.float32)
    joined_rows = jnp.concatenate([left_rows, local_rows, right_rows, spare_col], axis=2)
    flat_slots = neighbours.reshape(-1)
    stored_terms = []
    density_rows = []
    spare_rows = []
    for member in range(local_beads):
        gathered = joined_rows[:, member][:, neighbours]
        offset = positions[:, member][:, None, :] - gathered[:3]
        distance = jnp.sum(offset * offset, axis=0)
        density_term = jnp.exp(-alpha_shape * distance)
        repel_term = jnp.exp(-beta_shape * distance)
        collected = (
            jnp.zeros((slot_span + 1,), jnp.float32)
            .at[flat_slots]
            .add((amplitude[None, :] * density_term).reshape(-1))
        )
        density_rows.append(
            jnp.sum(gathered[3] * density_term, axis=0)
            + collected[ghost_count : ghost_count + atom_count]
        )
        spare_rows.append(
            jnp.concatenate(
                [collected[:ghost_count], collected[ghost_count + atom_count : slot_span]]
            )
        )
        stored_terms.append((offset, density_term, repel_term, gathered[3], gathered[4]))
    density = jnp.stack(density_rows)
    returned = with_halo(jnp.stack(spare_rows), (("slab", 1),), ghost_count)
    density = density.at[:, outgoing].add(
        jnp.concatenate([returned[:, :ghost_count], returned[:, 3 * ghost_count :]], axis=1)
    )
    slope_rows = -embedding[None, :] / (2.0 * jnp.sqrt(1.0 + density))
    slope_around = with_halo(jnp.take(slope_rows, outgoing, axis=1), (("slab", 1),), ghost_count)
    slope_ext = jnp.concatenate(
        [
            slope_around[:, :ghost_count],
            slope_rows,
            slope_around[:, 3 * ghost_count :],
            jnp.zeros((local_beads, 1), jnp.float32),
        ],
        axis=1,
    )
    force_rows = []
    spare_force = []
    for member in range(local_beads):
        offset, density_term, repel_term, partner_amp, partner_rep = stored_terms[member]
        coupling = 2.0 * (
            alpha_shape
            * density_term
            * (
                slope_rows[member][None, :] * partner_amp
                + slope_ext[member][neighbours] * amplitude[None, :]
            )
            + beta_shape * repulsion[None, :] * partner_rep * repel_term
        )
        pair_force = coupling[None] * offset
        collected = (
            jnp.zeros((3, slot_span + 1), jnp.float32)
            .at[:, flat_slots]
            .add(-pair_force.reshape(3, -1))
        )
        force_rows.append(
            jnp.sum(pair_force, axis=1) + collected[:, ghost_count : ghost_count + atom_count]
        )
        spare_force.append(
            jnp.concatenate(
                [collected[:, :ghost_count], collected[:, ghost_count + atom_count : slot_span]],
                axis=1,
            )
        )
    forces = jnp.stack(force_rows, axis=1)
    returned_force = with_halo(jnp.stack(spare_force, axis=1), (("slab", 2),), ghost_count)
    forces = forces.at[:, :, outgoing].add(
        jnp.concatenate(
            [returned_force[:, :, :ghost_count], returned_force[:, :, 3 * ghost_count :]], axis=2
        )
    )
    matrix = jnp.asarray(force_matrix(number), jnp.float32)
    new_accel = across_beads(forces, matrix) * inverse_mass[None, None, :]
    new_velocity = turned + 0.5 * step_dt * new_accel
    return (new_modes, new_velocity, new_accel)


def solution(mesh):
    return jax.shard_map(
        shards,
        mesh=mesh,
        in_specs=(
            P(None, "bead", "slab"),
            P(None, "bead", "slab"),
            P(None, "bead", "slab"),
            P("slab"),
            P(None, "slab"),
            P("slab", None),
        ),
        out_specs=(P(None, "bead", "slab"), P(None, "bead", "slab"), P(None, "bead", "slab")),
        check_vma=False,
    )
```

profile of v0, /device:TPU:0, one launch (start us, length us, event | category | flops | bytes accessed | tf_op | source)
XLA Modules:
  0.0 752.8 jit_solution(10489522635521770525)
XLA Ops:
  0.6 0.8 add_select_fusion
  1.7 1.3 reshape.421
  3.0 5.2 all-to-all-start
  8.1 0.7 broadcast_select_fusion.1
  8.8 0.7 fusion.24
  9.5 0.8 fusion.6
  10.4 0.9 copy.253
  11.4 2.8 gather_fusion.1
  14.3 0.7 and_select_fusion
  14.9 0.7 reduce
  15.6 0.5 broadcast.368
  16.2 0.7 reduce.7
  16.8 0.8 reshape.422
  17.8 0.8 convolution_bitcast_fusion.1
  18.7 0.6 copy.214
  19.3 4.2 all-to-all-start.1
  23.6 4.5 all-to-all-done.1
  28.5 2.0 gather_fusion
  31.4 3.6 collective-permute-start.1
  35.2 0.5 collective-permute-done
  35.7 0.6 collective-permute-done.1
  36.9 54.4 %gather_fusion.3 = f32[16384,5]{1,0:T(8,128)} fusion(f32[5,897]{0,1:T(8,128)S(1)} %bitcast.110, s32[16384]{0:T(1024)S(1)} %broadcast_clamp_fusion), kind=kCustom, calls=%fused_computation.3 | custom fusion | bytes 720896 | tf_op jit(solution)/shard_map/gather | solution.py:131
  91.3 5.3 copy.224
  96.8 54.4 %gather_fusion.2 = f32[16384,5]{1,0:T(8,128)} fusion(f32[5,897]{0,1:T(8,128)S(1)} %bitcast.111, s32[16384]{0:T(1024)S(1)} %broadcast_clamp_fusion), kind=kCustom, calls=%fused_computation.2 | custom fusion | bytes 720896 | tf_op jit(solution)/shard_map/gather | solution.py:131
  151.2 5.3 copy.221
  156.6 113.4 %scatter_custom_fusion.1 = f32[897]{0:T(1024)S(1)} fusion(s32[16384]{0:T(1024)S(1)} %bitcast.139, f32[16384]{0:T(1024)S(1)} %bitcast.143, f32[]{:T(128)} %constant.23.clone.1), kind=kCustom, calls=%fused_computation.94 | custom fusion | flops 16384 | bytes 3592 | tf_op jit(solution)/shard_map/scatter-add | solution.py:139
  270.3 113.4 %scatter_custom_fusion = f32[897]{0:T(1024)S(1)} fusion(s32[16384]{0:T(1024)S(1)} %bitcast.140, f32[16384]{0:T(1024)S(1)} %bitcast.144, f32[]{:T(128)} %constant.23.clone.1), kind=kCustom, calls=%fused_computation.96 | custom fusion | flops 16384 | bytes 3592 | tf_op jit(solution)/shard_map/scatter-add | solution.py:139
  383.9 3.6 collective-permute-start.3
  387.7 1.0 collective-permute-done.2
  389.0 2.7 scatter_fusion
  391.9 1.1 gather_fusion.4
  393.2 3.7 collective-permute-start.5
  397.4 2.1 collective-permute-done.4
  399.8 65.3 %gather_fusion.6 = f32[16384]{0:T(1024)S(1)} fusion(f32[897]{0:T(1024)S(1)} %bitcast.108, s32[16384]{0:T(1024)S(1)} %broadcast_clamp_fusion), kind=kCustom, calls=%fused_computation.6 | custom fusion | bytes 196608 | tf_op jit(solution)/shard_map/gather | solution.py:176
  465.1 65.3 %gather_fusion.5 = f32[16384]{0:T(1024)S(1)} fusion(f32[897]{0:T(1024)S(1)} %bitcast.107, s32[16384]{0:T(1024)S(1)} %broadcast_clamp_fusion), kind=kCustom, calls=%fused_computation.5 | custom fusion | bytes 196608 | tf_op jit(solution)/shard_map/gather | solution.py:176
  530.5 4.6 copy.247
  535.2 87.7 %scatter_custom_fusion.4 = f32[3,897]{0,1:T(8,128)S(1)} fusion(s32[16384]{0:T(1024)S(1)} %bitcast.141, f32[16384,3]{1,0:T(8,128)} %bitcast.115, f32[]{:T(128)} %constant.23.clone.1), kind=kCustom, calls=%fused_computation.24 | custom fusion | flops 49152 | bytes 11276 | tf_op jit(solution)/shard_map/scatter-add | solution.py:184
  623.2 4.6 copy.246
  627.9 87.7 %scatter_custom_fusion.3 = f32[3,897]{0,1:T(8,128)S(1)} fusion(s32[16384]{0:T(1024)S(1)} %bitcast.142, f32[16384,3]{1,0:T(8,128)} %bitcast.114, f32[]{:T(128)} %constant.23.clone.1), kind=kCustom, calls=%fused_computation.26 | custom fusion | flops 49152 | bytes 11276 | tf_op jit(solution)/shard_map/scatter-add | solution.py:184
  716.0 3.5 collective-permute-start.7
  720.4 0.5 collective-permute-done.6
  721.2 14.2 %scatter_fusion.1 = f32[3,2,512]{0,1,2:T(2,128)S(1)} fusion(f32[3,2,512]{0,1,2:T(2,128)S(1)} %copy.241, s32[384]{0:T(512)S(1)} %fusion.24, f32[384,3,2]{1,2,0:T(2,128)S(1)} %copy.242), kind=kCustom, calls=%fused_computation.12 | custom fusion | flops 2304 | bytes 29184 | tf_op jit(solution)/shard_map/scatter-add | solution.py:197
  735.5 0.6 reshape.423
  736.1 7.0 all_to_all.72
  743.1 0.7 reduce.8
  743.8 0.8 reshape.424
  745.0 7.1 all_to_all.73
  752.1 0.7 multiply_add_fusion
  (110 shorter events, 7.4 us)
Async XLA Ops:
  1.5 95.1 %copy-start.3 = (f32[3,2,512]{2,1,0:T(2,128)}, f32[3,2,512]{2,1,0:T(2,128)S(1)}, u32[]{:S(2)}) copy-start(f32[3,2,512]{2,1,0:T(2,128)S(1)} %add_select_fusion) | copy-start | bytes 36868
  3.0 12.7 %all-to-all-start = ((f32[4,1,768]{2,1,0:T(1,128)}), f32[4,1,768]{2,1,0:T(1,128)S(1)}, u32[]{:S(2)}, u32[]{:S(2)}) async-start(f32[4,1,768]{2,1,0:T(1,128)} %reshape.421), calls=%async_computation | async-start | bytes 24576 | tf_op jit(solution)/shard_map/all_to_all | solution.py:68
  19.3 8.9 %all-to-all-start.1 = ((f32[3,8,128]{2,0,1:T(4,128)}), f32[3,8,128]{2,0,1:T(4,128)S(1)}, u32[]{:S(2)}, u32[]{:S(2)}) async-start(f32[3,8,128]{2,0,1:T(4,128)} %copy.214), calls=%async_computation.1 | async-start | bytes 32768 | tf_op jit(solution)/shard_map/all_to_all | solution.py:71
  30.8 4.9 collective-permute-start
  31.4 4.9 collective-permute-start.1
  383.9 4.8 collective-permute-start.2
  383.9 4.9 collective-permute-start.3
  393.2 6.3 collective-permute-start.4
  393.2 6.4 collective-permute-start.5
  622.9 121.9 %copy-start.4 = (f32[8,8,1]{1,0,2:T(8,128)S(1)}, f32[8,8,1]{1,0,2:T(8,128)}, u32[]{:S(2)}) copy-start(f32[8,8,1]{1,0,2:T(8,128)} %constant.117) | copy-start | bytes 772
  623.0 129.1 %copy-start = (f32[3,2,512]{2,1,0:T(2,128)S(1)}, f32[3,2,512]{2,1,0:T(2,128)}, u32[]{:S(2)}) copy-start(f32[3,2,512]{2,1,0:T(2,128)} %param.8) | copy-start | bytes 36868
  623.0 129.1 %copy-start.1 = (f32[3,2,512]{2,1,0:T(2,128)S(1)}, f32[3,2,512]{2,1,0:T(2,128)}, u32[]{:S(2)}) copy-start(f32[3,2,512]{2,1,0:T(2,128)} %param.9) | copy-start | bytes 36868
  623.0 129.1 %copy-start.2 = (f32[3,2,512]{2,1,0:T(2,128)S(1)}, f32[3,2,512]{2,1,0:T(2,128)}, u32[]{:S(2)}) copy-start(f32[3,2,512]{2,1,0:T(2,128)} %param.10) | copy-start | bytes 36868
  716.0 4.9 collective-permute-start.6
  716.0 4.9 collective-permute-start.7
where the time goes:
time: 753 us
  other arithmetic  427 us (57%)
  local copies, waits for them, and re-layouts  276 us (37%)
  starting transfers between devices  23.9 us (3%)
  blocking collectives  14.1 us (2%)
  waiting for transfers between devices  9.35 us (1%)
    scatter-add x2, other arithmetic, shards(): collected = jnp.zeros((slot_span + 1,), jnp.float32).at[flat_slots].add((...  227 us
    scatter-add x2, other arithmetic, shards(): collected = jnp.zeros((3, slot_span + 1), jnp.float32).at[:, flat_slots]....  175 us
    gather x4, local copies, waits for them, and re-layouts, shards(): slope_ext[member][neighbours] * amplitude[None, :]  131 us
    gather x4, local copies, waits for them, and re-layouts, shards(): gathered = joined_rows[:, member][:, neighbours]  119 us
  transfers between devices with their start and end apart: 10, of which 7 were waited for; matrix products, arithmetic and copies ran while one was open for 1% of the time, Pallas kernels for 0%

commit v1 on v0

v1 whole, which is shorter than its diff:
```python
import functools
import math

import jax
import jax.numpy as jnp
import numpy as np
from jax import lax
from jax.experimental import pallas as pl
from jax.experimental.pallas import tpu as pltpu
from jax.sharding import PartitionSpec as P

step_dt = 0.1
spring = 6.0
alpha_shape = 0.3
beta_shape = 0.5
log2e = math.log2(math.e)
MESH = pl.DeviceIdType.MESH
f32 = jnp.float32
bf16 = jnp.bfloat16


def sectioning_inverse(number):
    row_table = np.zeros((number, number))
    row_table[0, 0] = 1.0
    for mode_level in range(number - 1, 0, -1):
        upper_row = row_table[0] if mode_level + 1 == number else row_table[mode_level + 1]
        row_table[mode_level] = (
            mode_level / (mode_level + 1.0) * upper_row + 1.0 / (mode_level + 1.0) * row_table[0]
        )
        row_table[mode_level, mode_level] += 1.0
    return row_table


def force_matrix(number):
    inverse = sectioning_inverse(number)
    weights = np.array([1.0] + [mode_level / (mode_level + 1.0) for mode_level in range(1, number)])
    return weights[:, None] * inverse.T / number


def split_rows(rows):
    high = rows.astype(bf16).astype(f32)
    rest = rows - high
    middle = rest.astype(bf16).astype(f32)
    return jnp.concatenate([high, middle, rest - middle], axis=0).astype(bf16)


def fold_pieces(product):
    return product[0:8] + product[8:16] + product[16:24]


def row_dot(rows, table):
    return fold_pieces(
        lax.dot_general(
            split_rows(rows), table, (((1,), (0,)), ((), ())), preferred_element_type=f32
        )
    )


def row_dot_nt(rows, table):
    return fold_pieces(
        lax.dot_general(
            split_rows(rows), table, (((1,), (1,)), ((), ())), preferred_element_type=f32
        )
    )


def lane_sums(selector, partial):
    high = partial.astype(bf16)
    rest = partial - high.astype(f32)
    middle = rest.astype(bf16)
    low = (rest - middle.astype(f32)).astype(bf16)
    total = None
    for piece in (high, middle, low):
        part = lax.dot_general(
            selector, piece, (((1,), (1,)), ((), ())), preferred_element_type=f32
        )
        total = part if total is None else total + part
    return total


def choose(index, table_values):
    value = f32(table_values[0])
    for i in range(1, len(table_values)):
        value = jnp.where(index == i, f32(table_values[i]), value)
    return value


def kernel(
    sizes,
    modes_ref,
    vel_ref,
    acc_ref,
    spec_ref,
    nb_ref,
    ghost_ref,
    out_modes,
    out_vel,
    out_acc,
    lo_ref,
    inc_ref,
    count_ref,
    turned_ref,
    onehot_ref,
    modes_all,
    send_modes,
    place_ref,
    column_ref,
    dens_ref,
    rep_ref,
    part_d,
    part_f,
    send_d,
    got_d,
    send_s,
    got_s,
    slope_ref,
    slope_col,
    send_f,
    force_all,
    mixed_ref,
    sem_a,
    rem_a,
    sem_b,
    rem_b,
    sem_c,
    rem_c,
    sem_f,
    rem_f,
):
    nbead, nslab, beads, atoms, ghosts, pad, slots = sizes
    number = nbead * beads
    b = lax.axis_index("bead")
    s = lax.axis_index("slab")
    left = lax.rem(s + nslab - 1, nslab)
    right = lax.rem(s + 1, nslab)

    barrier = pltpu.get_barrier_semaphore()
    peers = []
    for d in range(nbead):
        t = lax.rem(b + d, nbead)
        if d:
            peers.append((t, s))
        peers.append((t, left))
        peers.append((t, right))
    for peer in peers:
        pl.semaphore_signal(barrier, inc=1, device_id=peer, device_id_type=MESH)

    def remote(src, dst, sems, rems, index, device):
        return pltpu.make_async_remote_copy(
            src_ref=src,
            dst_ref=dst,
            send_sem=sems.at[index],
            recv_sem=rems.at[index],
            device_id=device,
            device_id_type=MESH,
        )

    shape = (3, beads, atoms)
    first_mode = (lax.broadcasted_iota(jnp.int32, shape, 1) + b * beads) == 0
    modes = modes_ref[...]
    half_kick = vel_ref[...] + 0.5 * step_dt * acc_ref[...]
    angle = spring * step_dt
    cosine, sine = math.cos(angle), math.sin(angle)
    new_modes = jnp.where(
        first_mode, modes + step_dt * half_kick, cosine * modes + sine / spring * half_kick
    )
    turned_ref[...] = jnp.where(
        first_mode, half_kick, cosine * half_kick - spring * sine * modes
    )
    out_modes[...] = new_modes
    heavy = spec_ref[...] == 1
    for c in range(3):
        modes_all[b, c * beads : (c + 1) * beads, 0:atoms] = new_modes[c]
    modes_all[b, 6:7, 0:atoms] = jnp.where(heavy, f32(1.4), f32(0.6))
    modes_all[b, 7:8, 0:atoms] = jnp.where(heavy, f32(1.5), f32(0.8))

    listed = ghost_ref[...]
    lane = lax.broadcasted_iota(jnp.int32, (1, pad), 1)
    first_list = jnp.where(lane < ghosts, listed[:, 0:pad], -1)
    start = 2 * ghosts - pad
    second_list = jnp.where(
        lane < ghosts,
        pltpu.roll(
            jnp.broadcast_to(listed[:, start : start + pad], (8, pad)),
            pad - (ghosts - start),
            1,
        )[0:1],
        -1,
    )
    atom_ids = lax.broadcasted_iota(jnp.int32, (atoms, pad), 0)
    onehot_ref[:, 0:pad] = jnp.where(atom_ids == first_list, f32(1), f32(0)).astype(bf16)
    onehot_ref[:, pad : 2 * pad] = jnp.where(atom_ids == second_list, f32(1), f32(0)).astype(bf16)
    send_modes[...] = row_dot(modes_all[b, :, 0:atoms], onehot_ref[...])

    pl.semaphore_wait(barrier, len(peers))

    left_at = slice(atoms, atoms + pad)
    right_at = slice(atoms + pad, atoms + 2 * pad)

    def exchange(own_ref, src_left, src_right, buffer, at_left, at_right, sems, rems):
        copies = []
        for d in range(nbead):
            t = lax.rem(b + d, nbead)
            copies.append(
                remote(src_left, buffer.at[b, :, at_left], sems, rems, nbead + d, (t, left))
            )
            copies.append(
                remote(src_right, buffer.at[b, :, at_right], sems, rems, 2 * nbead + d, (t, right))
            )
            if d:
                copies.append(
                    remote(own_ref, buffer.at[b, :, 0:atoms], sems, rems, d, (t, s))
                )
        for copy in copies:
            copy.start()
        return copies

    copies_a = exchange(
        modes_all.at[b, :, 0:atoms],
        send_modes.at[:, 0:pad],
        send_modes.at[:, pad : 2 * pad],
        modes_all,
        right_at,
        left_at,
        sem_a,
        rem_a,
    )

    rows = atoms + 2 * pad
    field = rows // 4
    value = nb_ref[...]
    moved = jnp.where(
        value < ghosts,
        value + atoms,
        jnp.where(value < ghosts + atoms, value - ghosts, value - ghosts + pad),
    )
    level = (
        jnp.where(moved >= field, 1, 0)
        + jnp.where(moved >= 2 * field, 1, 0)
        + jnp.where(moved >= 3 * field, 1, 0)
    )
    lo_ref[...] = moved - level * field
    step = jnp.where(
        level == 0, 1, jnp.where(level == 1, 1 << 8, jnp.where(level == 2, 1 << 16, 1 << 24))
    )
    inc_ref[...] = jnp.where(value < atoms + 2 * ghosts, step, 0)
    group = 32
    row_ids = lax.broadcasted_iota(jnp.int32, (group, atoms), 0)

    def count_body(g, carry):
        base = g * group
        total = jnp.zeros((group, atoms), jnp.int32)
        for k in range(slots):
            total = total + jnp.where(
                row_ids == lo_ref[k : k + 1, :] - base, inc_ref[k : k + 1, :], 0
            )
        for level_id in range(4):
            at = pl.multiple_of(level_id * field + base, group)
            count_ref[pl.ds(at, group), :] = (
                (total >> (8 * level_id)) & 255
            ).astype(f32)
        return carry

    lax.fori_loop(0, field // group, count_body, 0)

    for side in range(2):
        at = atoms + side * pad + ghosts
        blank = jnp.zeros((pad - ghosts, 128), f32)
        for kk in range(beads):
            part_d[kk, at : at + pad - ghosts, :] = blank
            for c in range(3):
                part_f[kk * 3 + c, at : at + pad - ghosts, :] = blank

    sub_ids = lax.broadcasted_iota(jnp.int32, (8, 1), 0)

    def mix(buffer, matrix, kk):
        total = None
        for n in range(nbead):
            column = None
            for j in range(beads):
                coef = choose(
                    b, [matrix[i * beads + kk, n * beads + j] for i in range(nbead)]
                )
                column = (
                    jnp.full((8, 1), coef, f32)
                    if column is None
                    else jnp.where(lax.rem(sub_ids, beads) == j, coef, column)
                )
            part = column * buffer[n]
            total = part if total is None else total + part
        result = total
        for j in range(1, beads):
            result = result + pltpu.roll(total, 8 - j, 0)
        return result

    inverse = sectioning_inverse(number).astype(np.float32)
    for copy in copies_a:
        copy.wait_recv()
    place_ref[6:8, :] = modes_all[b, 6:8, :]
    for kk in range(beads):
        mixed = mix(modes_all, inverse, kk)
        for c in range(3):
            place_ref[kk * 3 + c : kk * 3 + c + 1, :] = mixed[c * beads : c * beads + 1, :]
    column_ref[...] = jnp.transpose(place_ref[...])

    def rows_of(index):
        return jnp.broadcast_to(place_ref[index : index + 1, 0:atoms], (8, atoms))

    def fold_lanes(full):
        out = full[:, 0:128]
        for at in range(128, atoms, 128):
            out = out + full[:, at : at + 128]
        return out

    unroll = 2

    def density_pass(kk, first_row, count, total):
        xn = [rows_of(kk * 3 + c) for c in range(3)]
        amp_n, rep_n = rows_of(6), rows_of(7)

        def body(i, total):
            for u in range(unroll):
                at = pl.multiple_of(first_row + (i * unroll + u) * 8, 8)
                here = pl.ds(at, 8)
                cols = column_ref[here, :]
                offset = [xn[c] - cols[:, kk * 3 + c : kk * 3 + c + 1] for c in range(3)]
                distance = (
                    offset[0] * offset[0] + offset[1] * offset[1] + offset[2] * offset[2]
                )
                listed_times = count_ref[here, :]
                dens = listed_times * jnp.exp2((-alpha_shape * log2e) * distance)
                repel = listed_times * jnp.exp2((-beta_shape * log2e) * distance)
                dens_ref[kk, here, :] = dens
                rep_ref[kk, here, :] = repel * (rep_n * cols[:, 7:8])
                part_d[kk, here, :] = fold_lanes(dens * amp_n)
                total = total + dens * cols[:, 6:7]
            return total

        return lax.fori_loop(0, count // (8 * unroll), body, total)

    ones = jnp.ones((8, 128), bf16)
    sides = (slice(atoms, atoms + pad), slice(atoms + pad, atoms + 2 * pad))
    totals = []
    copies_b = []
    for kk in range(beads):
        total = jnp.zeros((8, atoms), f32)
        for side in range(2):
            total = density_pass(kk, atoms + side * pad, ghosts, total)
            send_d[kk, :, side * pad : (side + 1) * pad] = lane_sums(
                ones, part_d[kk, sides[side], :]
            )
        pair = [
            remote(
                send_d.at[kk, :, 0:pad],
                got_d.at[kk, :, pad : 2 * pad],
                sem_b,
                rem_b,
                2 * kk,
                (b, left),
            ),
            remote(
                send_d.at[kk, :, pad : 2 * pad],
                got_d.at[kk, :, 0:pad],
                sem_b,
                rem_b,
                2 * kk + 1,
                (b, right),
            ),
        ]
        for copy in pair:
            copy.start()
        copies_b.append(pair)
        totals.append(total)
    locals_d = []
    for kk in range(beads):
        total = density_pass(kk, 0, atoms, totals[kk])
        locals_d.append(
            jnp.sum(total, axis=0, keepdims=True) + lane_sums(ones, part_d[kk, 0:atoms, :])
        )
    embed = jnp.where(heavy, f32(2.5), f32(1.0))
    copies_c = []
    for kk in range(beads):
        for copy in copies_b[kk]:
            copy.wait_recv()
        density = locals_d[kk] + row_dot_nt(got_d[kk], onehot_ref[...])
        slope = (-0.5 * 2.0 * alpha_shape) * embed / jnp.sqrt(1.0 + density)
        slope_ref[kk] = slope
        send_s[kk] = row_dot(slope, onehot_ref[...])
        pair = [
            remote(
                send_s.at[kk, :, 0:pad],
                got_s.at[kk, :, pad : 2 * pad],
                sem_c,
                rem_c,
                2 * kk,
                (b, left),
            ),
            remote(
                send_s.at[kk, :, pad : 2 * pad],
                got_s.at[kk, :, 0:pad],
                sem_c,
                rem_c,
                2 * kk + 1,
                (b, right),
            ),
        ]
        for copy in pair:
            copy.start()
        copies_c.append(pair)
        slope_col[kk, 0:atoms, :] = jnp.transpose(slope)

    def force_pass(kk, first_row, count, carry):
        xn = [rows_of(kk * 3 + c) for c in range(3)]
        amp_n = rows_of(6)
        slope_n = slope_ref[kk]

        def body(i, totals):
            for u in range(unroll):
                at = pl.multiple_of(first_row + (i * unroll + u) * 8, 8)
                here = pl.ds(at, 8)
                cols = column_ref[here, :]
                slope_m = slope_col[kk, here, :][:, 0:1]
                coupling = (
                    dens_ref[kk, here, :] * (slope_n * cols[:, 6:7] + amp_n * slope_m)
                    + rep_ref[kk, here, :]
                )
                out = []
                for c in range(3):
                    pair_force = coupling * (xn[c] - cols[:, kk * 3 + c : kk * 3 + c + 1])
                    part_f[kk * 3 + c, here, :] = fold_lanes(pair_force)
                    out.append(totals[c] + pair_force)
                totals = tuple(out)
            return totals

        return lax.fori_loop(0, count // (8 * unroll), body, carry)

    selector_ids = lax.broadcasted_iota(jnp.int32, (8, 128), 0)
    line_ids = lax.broadcasted_iota(jnp.int32, (8, atoms), 0)
    zero = jnp.zeros((8, atoms), f32)
    local_totals = [force_pass(kk, 0, atoms, (zero, zero, zero)) for kk in range(beads)]
    own = zero
    for kk in range(beads):
        for copy in copies_c[kk]:
            copy.wait_recv()
        slope_col[kk, atoms:rows, :] = jnp.transpose(got_s[kk])
        total = local_totals[kk]
        for side in range(2):
            total = force_pass(kk, atoms + side * pad, ghosts, total)
        for c in range(3):
            line = jnp.sum(total[c], axis=0, keepdims=True)
            own = own + jnp.where(line_ids == c * beads + kk, line, 0.0)
    sent = jnp.zeros((8, rows), f32)
    for kk in range(beads):
        for c in range(3):
            selector = jnp.where(selector_ids == c * beads + kk, f32(-1), f32(0)).astype(bf16)
            sent = sent + lane_sums(selector, part_f[kk * 3 + c])
    force_all[b, :, 0:atoms] = own + sent[:, 0:atoms]
    send_f[...] = sent[:, atoms:rows]
    copies_f = exchange(
        force_all.at[b, :, 0:atoms],
        send_f.at[:, 0:pad],
        send_f.at[:, pad : 2 * pad],
        force_all,
        right_at,
        left_at,
        sem_f,
        rem_f,
    )
    for copy in copies_a:
        copy.wait_send()
    for copy in sum(copies_b, []) + sum(copies_c, []):
        copy.wait_send()
    matrix = force_matrix(number).astype(np.float32)
    inverse_mass = jnp.where(heavy, f32(1.0 / 106.0), f32(1.0))
    for copy in copies_f:
        copy.wait_recv()
    mixed_ref[6:8, :] = jnp.zeros((2, rows), f32)
    for kk in range(beads):
        mixed = mix(force_all, matrix, kk)
        for c in range(3):
            at = c * beads + kk
            mixed_ref[at : at + 1, :] = mixed[c * beads : c * beads + 1, :]
    accel = (
        mixed_ref[:, 0:atoms] + row_dot_nt(mixed_ref[:, atoms:rows], onehot_ref[...])
    ) * inverse_mass
    for c in range(3):
        piece = accel[c * beads : (c + 1) * beads]
        out_acc[c] = piece
        out_vel[c] = turned_ref[c] + 0.5 * step_dt * piece
    for copy in copies_f:
        copy.wait_send()


def shards(section_modes, velocity, acceleration, species, neighbours, ghost_send):
    _, beads, atoms = section_modes.shape
    slots = neighbours.shape[0]
    ghosts = ghost_send.shape[1] // 2
    pad = -(-ghosts // 128) * 128
    rows = atoms + 2 * pad
    nbead, nslab = lax.axis_size("bead"), lax.axis_size("slab")
    sizes = (nbead, nslab, beads, atoms, ghosts, pad, slots)
    vmem = pl.BlockSpec(memory_space=pltpu.VMEM)
    result = jax.ShapeDtypeStruct(section_modes.shape, f32)
    dma = pltpu.SemaphoreType.DMA
    return pl.pallas_call(
        functools.partial(kernel, sizes),
        out_shape=(result, result, result),
        in_specs=[vmem] * 6,
        out_specs=(vmem, vmem, vmem),
        scratch_shapes=[
            pltpu.VMEM((slots, atoms), jnp.int32),
            pltpu.VMEM((slots, atoms), jnp.int32),
            pltpu.VMEM((rows, atoms), f32),
            pltpu.VMEM((3, beads, atoms), f32),
            pltpu.VMEM((atoms, 2 * pad), bf16),
            pltpu.VMEM((nbead, 8, rows), f32),
            pltpu.VMEM((8, 2 * pad), f32),
            pltpu.VMEM((8, rows), f32),
            pltpu.VMEM((rows, 8), f32),
            pltpu.VMEM((beads, rows, atoms), f32),
            pltpu.VMEM((beads, rows, atoms), f32),
            pltpu.VMEM((beads, rows, 128), f32),
            pltpu.VMEM((beads * 3, rows, 128), f32),
            pltpu.VMEM((beads, 8, 2 * pad), f32),
            pltpu.VMEM((beads, 8, 2 * pad), f32),
            pltpu.VMEM((beads, 8, 2 * pad), f32),
            pltpu.VMEM((beads, 8, 2 * pad), f32),
            pltpu.VMEM((beads, 8, atoms), f32),
            pltpu.VMEM((beads, rows, 8), f32),
            pltpu.VMEM((8, 2 * pad), f32),
            pltpu.VMEM((nbead, 8, rows), f32),
            pltpu.VMEM((8, rows), f32),
            dma((3 * nbead,)),
            dma((3 * nbead,)),
            dma((2 * beads,)),
            dma((2 * beads,)),
            dma((2 * beads,)),
            dma((2 * beads,)),
            dma((3 * nbead,)),
            dma((3 * nbead,)),
        ],
        compiler_params=pltpu.CompilerParams(
            collective_id=0, has_side_effects=True, vmem_limit_bytes=40 * 1024 * 1024
        ),
    )(
        section_modes,
        velocity,
        acceleration,
        species.reshape(1, atoms),
        neighbours,
        ghost_send,
    )


def solution(mesh):
    return jax.shard_map(
        shards,
        mesh=mesh,
        in_specs=(
            P(None, "bead", "slab"),
            P(None, "bead", "slab"),
            P(None, "bead", "slab"),
            P("slab"),
            P(None, "slab"),
            P("slab", None),
        ),
        out_specs=(P(None, "bead", "slab"), P(None, "bead", "slab"), P(None, "bead", "slab")),
        check_vma=False,
    )
```

time: 753 us -> 47.9 us (0.06)
  other arithmetic: 427 us -> 0 us
  local copies, waits for them, and re-layouts: 276 us -> 6.11 us
  Pallas kernels: 0 us -> 40.7 us
  starting transfers between devices: 23.9 us -> 0 us
  blocking collectives: 14.1 us -> 0 us
  waiting for transfers between devices: 9.35 us -> 0 us
    scatter-add x6 -> x0, other arithmetic: 419 us -> none  [the longest x2 227 us: shards(): collected = jnp.zeros((slot_span + 1,), jnp.float32).at[flat_slots].add((...]
    gather x13 -> x0, local copies, waits for them, and re-layouts: 256 us -> none  [the longest x4 131 us: shards(): slope_ext[member][neighbours] * amplitude[None, :]]
    pallas_call x0 -> x1, Pallas kernels: none -> 40.7 us  [shards(): pl.pallas_call(functools.partial(kernel, sizes), out_shape=(result, resul...]
    ppermute x8 -> x0, starting transfers between devices: 14.5 us -> none  [the longest x4 14.4 us: with_halo(): after = lax.ppermute(leading, axis, down)]
    all_to_all x2 -> x0, blocking collectives: 14.1 us -> none  [the longest x1 7.06 us: across_beads(): lax.all_to_all(mixed_rows, 'bead', split_axis=1, concat_axis=2, tiled=True)]
    all_to_all x2 -> x0, starting transfers between devices: 9.36 us -> none  [the longest x1 5.16 us: across_beads(): lax.all_to_all(values, 'bead', split_axis=2, concat_axis=1, tiled=True)]
    neg x2 -> x0, local copies, waits for them, and re-layouts: 9.29 us -> none  [shards(): -pair_force.reshape(3, -1)]
  transfers between devices with their start and end apart: 10 -> 0, of which waited for: 7 -> 0; matrix products, arithmetic and copies ran while one was open for 1% -> 0% of each run, Pallas kernels for 0% -> 0%
where the time goes in v1:
time: 47.9 us; the launch traced here: 47.5 us
  Pallas kernels  40.7 us (85%)
  local copies, waits for them, and re-layouts  6.11 us (13%)
  between operations  0.65 us (1%)
    pallas_call x1, Pallas kernels, shards(): pl.pallas_call(functools.partial(kernel, sizes), out_shape=(result, resul...  40.7 us
    unnamed x15, local copies, waits for them, and re-layouts  6.11 us

profile of v1, /device:TPU:0, one launch (start us, length us, event | category | flops | bytes accessed | tf_op | source)
XLA Modules:
  0.0 47.5 jit_solution(17213623318220433546)
XLA Ops:
  0.6 0.0 copy-start.5
  0.6 0.7 %copy-done.5 = s32[1,384]{1,0:T(1,128)S(1)} copy-done((s32[1,384]{1,0:T(1,128)S(1)}, s32[1,384]{1,0:T(1,128)}, u32[]{:S(2)}) %copy-start.5) | copy-done | bytes 1560
  1.3 0.0 copy-start
  1.3 0.8 %copy-done = s32[32,512]{1,0:T(8,128)S(1)} copy-done((s32[32,512]{1,0:T(8,128)S(1)}, s32[32,512]{1,0:T(8,128)}, u32[]{:S(2)}) %copy-start) | copy-done | bytes 65560
  2.2 0.0 copy-start.1
  2.2 0.7 %copy-done.1 = f32[3,2,512]{2,1,0:T(2,128)S(1)} copy-done((f32[3,2,512]{2,1,0:T(2,128)S(1)}, f32[3,2,512]{2,1,0:T(2,128)}, u32[]{:S(2)}) %copy-start.1) | copy-done | bytes 12312
  2.9 0.0 copy-start.2
  2.9 0.7 %copy-done.2 = f32[3,2,512]{2,1,0:T(2,128)S(1)} copy-done((f32[3,2,512]{2,1,0:T(2,128)S(1)}, f32[3,2,512]{2,1,0:T(2,128)}, u32[]{:S(2)}) %copy-start.2) | copy-done | bytes 12312
  3.6 0.0 copy-start.3
  3.6 0.7 %copy-done.3 = f32[3,2,512]{2,1,0:T(2,128)S(1)} copy-done((f32[3,2,512]{2,1,0:T(2,128)S(1)}, f32[3,2,512]{2,1,0:T(2,128)}, u32[]{:S(2)}) %copy-start.3) | copy-done | bytes 12312
  4.3 0.0 copy-start.4
  4.3 0.7 %copy-done.4 = s32[512]{0:T(512)S(1)} copy-done((s32[512]{0:T(512)S(1)}, s32[512]{0:T(512)}, u32[]{:S(2)}) %copy-start.4) | copy-done | bytes 2072
  5.0 40.7 %shard_map.85 = (f32[3,2,512]{2,1,0:T(2,128)S(1)}, f32[3,2,512]{2,1,0:T(2,128)S(1)}, f32[3,2,512]{2,1,0:T(2,128)S(1)}) custom-call(f32[3,2,512]{2,1,0:T(2,128)S(1)} %copy-done.1, f32[3,2,512]{2,1,0:T(2,128)S(1)} %copy-done.2, f32[3,2,512]{2,1,0:T(2,128)S(1)} %copy-done.3, s32[1,512]{1,0:T(1,128)S(1)} %bitcast.1, s32[32,512]{1,0:T(8,128)S(1)} %copy-done, ...), custom_call_target="tpu_custom_call" | custom-call | tf_op jit(solution)/shard_map/pallas_call | solution.py:505
  45.7 0.6 %copy.12 = f32[3,2,512]{2,1,0:T(2,128)} copy(f32[3,2,512]{2,1,0:T(2,128)S(1)} %get-tuple-element.6) | data formatting | bytes 24576
  46.3 0.6 %copy.13 = f32[3,2,512]{2,1,0:T(2,128)} copy(f32[3,2,512]{2,1,0:T(2,128)S(1)} %get-tuple-element.7) | data formatting | bytes 24576
  46.9 0.6 %copy.14 = f32[3,2,512]{2,1,0:T(2,128)} copy(f32[3,2,512]{2,1,0:T(2,128)S(1)} %get-tuple-element.8) | data formatting | bytes 24576
Async XLA Ops:
  0.6 0.7 %copy-start.5 = (s32[1,384]{1,0:T(1,128)S(1)}, s32[1,384]{1,0:T(1,128)}, u32[]{:S(2)}) copy-start(s32[1,384]{1,0:T(1,128)} %ghost_ref.1) | copy-start | bytes 4612
  1.3 0.8 %copy-start = (s32[32,512]{1,0:T(8,128)S(1)}, s32[32,512]{1,0:T(8,128)}, u32[]{:S(2)}) copy-start(s32[32,512]{1,0:T(8,128)} %nb_ref.1) | copy-start | bytes 196612
  2.2 0.7 %copy-start.1 = (f32[3,2,512]{2,1,0:T(2,128)S(1)}, f32[3,2,512]{2,1,0:T(2,128)}, u32[]{:S(2)}) copy-start(f32[3,2,512]{2,1,0:T(2,128)} %modes_ref.1) | copy-start | bytes 36868
  2.9 0.7 %copy-start.2 = (f32[3,2,512]{2,1,0:T(2,128)S(1)}, f32[3,2,512]{2,1,0:T(2,128)}, u32[]{:S(2)}) copy-start(f32[3,2,512]{2,1,0:T(2,128)} %vel_ref.1) | copy-start | bytes 36868
  3.6 0.7 %copy-start.3 = (f32[3,2,512]{2,1,0:T(2,128)S(1)}, f32[3,2,512]{2,1,0:T(2,128)}, u32[]{:S(2)}) copy-start(f32[3,2,512]{2,1,0:T(2,128)} %acc_ref.1) | copy-start | bytes 36868
  4.3 0.7 %copy-start.4 = (s32[512]{0:T(512)S(1)}, s32[512]{0:T(512)}, u32[]{:S(2)}) copy-start(s32[512]{0:T(512)} %param.9) | copy-start | bytes 6148

commit v2 on v1

--- a/solution.py
+++ b/solution.py
@@ -87,15 +87,22 @@
 
 def kernel(
     sizes,
+    modes_in,
+    vel_in,
+    acc_in,
+    spec_in,
+    nb_in,
+    ghost_in,
+    out_modes,
+    out_vel,
+    out_acc,
     modes_ref,
     vel_ref,
     acc_ref,
     spec_ref,
     nb_ref,
     ghost_ref,
-    out_modes,
-    out_vel,
-    out_acc,
+    sem_in,
     lo_ref,
     inc_ref,
     count_ref,
@@ -134,6 +141,21 @@
     left = lax.rem(s + nslab - 1, nslab)
     right = lax.rem(s + 1, nslab)
 
+    loads = [
+        pltpu.make_async_copy(src, dst, sem_in.at[i])
+        for i, (src, dst) in enumerate(
+            (
+                (modes_in, modes_ref),
+                (vel_in, vel_ref),
+                (acc_in, acc_ref),
+                (spec_in, spec_ref),
+                (ghost_in, ghost_ref),
+                (nb_in, nb_ref),
+            )
+        )
+    ]
+    for load in loads:
+        load.start()
     barrier = pltpu.get_barrier_semaphore()
     peers = []
     for d in range(nbead):
@@ -155,6 +177,8 @@
             device_id_type=MESH,
         )
 
+    for load in loads[:5]:
+        load.wait()
     shape = (3, beads, atoms)
     first_mode = (lax.broadcasted_iota(jnp.int32, shape, 1) + b * beads) == 0
     modes = modes_ref[...]
@@ -228,6 +252,7 @@
 
     rows = atoms + 2 * pad
     field = rows // 4
+    loads[5].wait()
     value = nb_ref[...]
     moved = jnp.where(
         value < ghosts,
@@ -312,7 +337,7 @@
             out = out + full[:, at : at + 128]
         return out
 
-    unroll = 2
+    unroll = 8
 
     def density_pass(kk, first_row, count, total):
         xn = [rows_of(kk * 3 + c) for c in range(3)]
@@ -491,6 +516,17 @@
         copy.wait_send()
 
 
+def store_kernel(a_in, b_in, c_in, a_out, b_out, c_out, sems):
+    copies = [
+        pltpu.make_async_copy(src, dst, sems.at[i])
+        for i, (src, dst) in enumerate(((a_in, a_out), (b_in, b_out), (c_in, c_out)))
+    ]
+    for copy in copies:
+        copy.start()
+    for copy in copies:
+        copy.wait()
+
+
 def shards(section_modes, velocity, acceleration, species, neighbours, ghost_send):
     _, beads, atoms = section_modes.shape
     slots = neighbours.shape[0]
@@ -502,12 +538,19 @@
     vmem = pl.BlockSpec(memory_space=pltpu.VMEM)
     result = jax.ShapeDtypeStruct(section_modes.shape, f32)
     dma = pltpu.SemaphoreType.DMA
-    return pl.pallas_call(
+    results = pl.pallas_call(
         functools.partial(kernel, sizes),
         out_shape=(result, result, result),
-        in_specs=[vmem] * 6,
+        in_specs=[pl.BlockSpec(memory_space=pltpu.HBM)] * 6,
         out_specs=(vmem, vmem, vmem),
         scratch_shapes=[
+            pltpu.VMEM(section_modes.shape, f32),
+            pltpu.VMEM(section_modes.shape, f32),
+            pltpu.VMEM(section_modes.shape, f32),
+            pltpu.VMEM((1, atoms), jnp.int32),
+            pltpu.VMEM((slots, atoms), jnp.int32),
+            pltpu.VMEM((1, 2 * ghosts), jnp.int32),
+            dma((6,)),
             pltpu.VMEM((slots, atoms), jnp.int32),
             pltpu.VMEM((slots, atoms), jnp.int32),
             pltpu.VMEM((rows, atoms), f32),
@@ -540,7 +583,7 @@
             dma((3 * nbead,)),
         ],
         compiler_params=pltpu.CompilerParams(
-            collective_id=0, has_side_effects=True, vmem_limit_bytes=40 * 1024 * 1024
+            collective_id=0, has_side_effects=True, vmem_limit_bytes=64 * 1024 * 1024
         ),
     )(
         section_modes,
@@ -550,6 +593,14 @@
         neighbours,
         ghost_send,
     )
+    return pl.pallas_call(
+        store_kernel,
+        out_shape=(result, result, result),
+        in_specs=[vmem] * 3,
+        out_specs=[pl.BlockSpec(memory_space=pltpu.HBM)] * 3,
+        scratch_shapes=[dma((3,))],
+        compiler_params=pltpu.CompilerParams(vmem_limit_bytes=64 * 1024 * 1024),
+    )(*results)
 
 
 def solution(mesh):

time: 47.9 us -> 31.7 us (0.66)
  Pallas kernels: 40.7 us -> 30.8 us
  local copies, waits for them, and re-layouts: 6.11 us -> 0 us
    pallas_call x1, Pallas kernels: 40.7 us -> 29.4 us  [shards(): pl.pallas_call(functools.partial(kernel, sizes), out_shape=(result, resul...]
    unnamed x15 -> x0, local copies, waits for them, and re-layouts: 6.11 us -> none
    pallas_call x0 -> x1, Pallas kernels: none -> 1.37 us  [shards(): pl.pallas_call(store_kernel, out_shape=(result, result, result), in_specs...]
where the time goes in v2:
time: 31.7 us; the launch traced here: 31.4 us
  Pallas kernels  30.8 us (97%)
  between operations  0.64 us (2%)
    pallas_call x1, Pallas kernels, shards(): pl.pallas_call(functools.partial(kernel, sizes), out_shape=(result, resul...  29.4 us
    pallas_call x1, Pallas kernels, shards(): pl.pallas_call(store_kernel, out_shape=(result, result, result), in_specs...  1.37 us

profile of v2, /device:TPU:0, one launch (start us, length us, event | category | flops | bytes accessed | tf_op | source)
XLA Modules:
  0.0 31.4 jit_solution(5526345567300325493)
XLA Ops:
  0.6 29.4 %shard_map.85 = (f32[3,2,512]{2,1,0:T(2,128)}, f32[3,2,512]{2,1,0:T(2,128)}, f32[3,2,512]{2,1,0:T(2,128)}) custom-call(f32[3,2,512]{2,1,0:T(2,128)} %modes_in.1, f32[3,2,512]{2,1,0:T(2,128)} %vel_in.1, f32[3,2,512]{2,1,0:T(2,128)} %acc_in.1, s32[1,512]{1,0:T(1,128)} %bitcast.1, s32[32,512]{1,0:T(8,128)} %nb_in.1, s32[1,384]{1,0:T(1,128)} %ghost_in.1), custom_call_target="tpu_custom_call" | custom-call | tf_op jit(solution)/shard_map/pallas_call | solution.py:541
  30.0 1.4 %shard_map.86 = (f32[3,2,512]{2,1,0:T(2,128)}, f32[3,2,512]{2,1,0:T(2,128)}, f32[3,2,512]{2,1,0:T(2,128)}) custom-call(f32[3,2,512]{2,1,0:T(2,128)} %get-tuple-element.6.a_in, f32[3,2,512]{2,1,0:T(2,128)} %get-tuple-element.7.b_in, f32[3,2,512]{2,1,0:T(2,128)} %get-tuple-element.8.c_in), custom_call_target="tpu_custom_call" | custom-call | tf_op jit(solution)/shard_map/pallas_call | solution.py:596

commit v3 on v2

--- a/solution.py
+++ b/solution.py
@@ -68,9 +68,8 @@
     high = partial.astype(bf16)
     rest = partial - high.astype(f32)
     middle = rest.astype(bf16)
-    low = (rest - middle.astype(f32)).astype(bf16)
     total = None
-    for piece in (high, middle, low):
+    for piece in (high, middle):
         part = lax.dot_general(
             selector, piece, (((1,), (1,)), ((), ())), preferred_element_type=f32
         )
@@ -298,8 +297,8 @@
 
     sub_ids = lax.broadcasted_iota(jnp.int32, (8, 1), 0)
 
-    def mix(buffer, matrix, kk):
-        total = None
+    def mix_columns(matrix, kk):
+        columns = []
         for n in range(nbead):
             column = None
             for j in range(beads):
@@ -311,7 +310,13 @@
                     if column is None
                     else jnp.where(lax.rem(sub_ids, beads) == j, coef, column)
                 )
-            part = column * buffer[n]
+            columns.append(column)
+        return columns
+
+    def mix(buffer, columns):
+        total = None
+        for n in range(nbead):
+            part = columns[n] * buffer[n]
             total = part if total is None else total + part
         result = total
         for j in range(1, beads):
@@ -319,11 +324,12 @@
         return result
 
     inverse = sectioning_inverse(number).astype(np.float32)
+    inverse_columns = [mix_columns(inverse, kk) for kk in range(beads)]
     for copy in copies_a:
         copy.wait_recv()
     place_ref[6:8, :] = modes_all[b, 6:8, :]
     for kk in range(beads):
-        mixed = mix(modes_all, inverse, kk)
+        mixed = mix(modes_all, inverse_columns[kk])
         for c in range(3):
             place_ref[kk * 3 + c : kk * 3 + c + 1, :] = mixed[c * beads : c * beads + 1, :]
     column_ref[...] = jnp.transpose(place_ref[...])
@@ -340,6 +346,7 @@
     unroll = 8
 
     def density_pass(kk, first_row, count, total):
+        unroll = 32 if count % 256 == 0 else 24 if count % 192 == 0 else 8
         xn = [rows_of(kk * 3 + c) for c in range(3)]
         amp_n, rep_n = rows_of(6), rows_of(7)
 
@@ -435,6 +442,7 @@
         slope_col[kk, 0:atoms, :] = jnp.transpose(slope)
 
     def force_pass(kk, first_row, count, carry):
+        unroll = 32 if count % 256 == 0 else 24 if count % 192 == 0 else 8
         xn = [rows_of(kk * 3 + c) for c in range(3)]
         amp_n = rows_of(6)
         slope_n = slope_ref[kk]
@@ -463,7 +471,14 @@
     line_ids = lax.broadcasted_iota(jnp.int32, (8, atoms), 0)
     zero = jnp.zeros((8, atoms), f32)
     local_totals = [force_pass(kk, 0, atoms, (zero, zero, zero)) for kk in range(beads)]
-    own = zero
+    def lane_rows(at, into):
+        for kk in range(beads):
+            for c in range(3):
+                selector = jnp.where(selector_ids == c * beads + kk, f32(-1), f32(0)).astype(bf16)
+                into = into + lane_sums(selector, part_f[kk * 3 + c, at, :])
+        return into
+
+    own = lane_rows(slice(0, atoms), zero)
     for kk in range(beads):
         for copy in copies_c[kk]:
             copy.wait_recv()
@@ -474,13 +489,8 @@
         for c in range(3):
             line = jnp.sum(total[c], axis=0, keepdims=True)
             own = own + jnp.where(line_ids == c * beads + kk, line, 0.0)
-    sent = jnp.zeros((8, rows), f32)
-    for kk in range(beads):
-        for c in range(3):
-            selector = jnp.where(selector_ids == c * beads + kk, f32(-1), f32(0)).astype(bf16)
-            sent = sent + lane_sums(selector, part_f[kk * 3 + c])
-    force_all[b, :, 0:atoms] = own + sent[:, 0:atoms]
-    send_f[...] = sent[:, atoms:rows]
+    force_all[b, :, 0:atoms] = own
+    send_f[...] = lane_rows(slice(atoms, rows), jnp.zeros((8, 2 * pad), f32))
     copies_f = exchange(
         force_all.at[b, :, 0:atoms],
         send_f.at[:, 0:pad],
@@ -496,12 +506,13 @@
     for copy in sum(copies_b, []) + sum(copies_c, []):
         copy.wait_send()
     matrix = force_matrix(number).astype(np.float32)
+    force_columns = [mix_columns(matrix, kk) for kk in range(beads)]
     inverse_mass = jnp.where(heavy, f32(1.0 / 106.0), f32(1.0))
     for copy in copies_f:
         copy.wait_recv()
     mixed_ref[6:8, :] = jnp.zeros((2, rows), f32)
     for kk in range(beads):
-        mixed = mix(force_all, matrix, kk)
+        mixed = mix(force_all, force_columns[kk])
         for c in range(3):
             at = c * beads + kk
             mixed_ref[at : at + 1, :] = mixed[c * beads : c * beads + 1, :]

time: 31.7 us -> 28.1 us (0.89)
  Pallas kernels: 30.8 us -> 27.2 us
    pallas_call x1, Pallas kernels: 29.4 us -> 25.8 us  [shards(): pl.pallas_call(functools.partial(kernel, sizes), out_shape=(result, resul...]
where the time goes in v3:
time: 28.1 us; the launch traced here: 27.8 us
  Pallas kernels  27.2 us (97%)
  between operations  0.64 us (2%)
    pallas_call x1, Pallas kernels, shards(): pl.pallas_call(functools.partial(kernel, sizes), out_shape=(result, resul...  25.8 us
    pallas_call x1, Pallas kernels, shards(): pl.pallas_call(store_kernel, out_shape=(result, result, result), in_specs...  1.37 us

profile of v3, /device:TPU:0, one launch (start us, length us, event | category | flops | bytes accessed | tf_op | source)
XLA Modules:
  0.0 27.8 jit_solution(7577736643734952375)
XLA Ops:
  0.6 25.8 %shard_map.85 = (f32[3,2,512]{2,1,0:T(2,128)}, f32[3,2,512]{2,1,0:T(2,128)}, f32[3,2,512]{2,1,0:T(2,128)}) custom-call(f32[3,2,512]{2,1,0:T(2,128)} %modes_in.1, f32[3,2,512]{2,1,0:T(2,128)} %vel_in.1, f32[3,2,512]{2,1,0:T(2,128)} %acc_in.1, s32[1,512]{1,0:T(1,128)} %bitcast.1, s32[32,512]{1,0:T(8,128)} %nb_in.1, s32[1,384]{1,0:T(1,128)} %ghost_in.1), custom_call_target="tpu_custom_call" | custom-call | tf_op jit(solution)/shard_map/pallas_call | solution.py:552
  26.4 1.4 %shard_map.86 = (f32[3,2,512]{2,1,0:T(2,128)}, f32[3,2,512]{2,1,0:T(2,128)}, f32[3,2,512]{2,1,0:T(2,128)}) custom-call(f32[3,2,512]{2,1,0:T(2,128)} %get-tuple-element.6.a_in, f32[3,2,512]{2,1,0:T(2,128)} %get-tuple-element.7.b_in, f32[3,2,512]{2,1,0:T(2,128)} %get-tuple-element.8.c_in), custom_call_target="tpu_custom_call" | custom-call | tf_op jit(solution)/shard_map/pallas_call | solution.py:607
